TPU v7x, 32 devices: a whole 2x2x4 slice. The times are simulated.
32 devices in a mesh: tm: 16 (over z, y, x), dp: 2 (over core).
Axes of the slice: x: 2, y: 2, z: 4, core: 2. Of those that a mesh axis runs over, the one named last changes fastest.
Arguments:
- frame_tokens: bfloat16 [2, 48, 64, 1280], P('dp', 'tm'), may hold values from -8 to 8
- visible: int32 [2, 48, 64], P('dp'), may hold values from 0 to 2
- grad_output: bfloat16 [2, 48, 64, 1280], P('dp', 'tm'), may hold values from -6 to 6
- norm_gain: float32 [1280], replicated, may hold values from 0.1 to 1.9
- query_weight: bfloat16 [1280, 640], P('tm'), may hold values from -1.5 to 1.5
- key_weight: bfloat16 [1280, 640], P('tm'), may hold values from -1.5 to 1.5
- value_weight: bfloat16 [1280, 640], P('tm'), may hold values from -0.15625 to 0.15625
- output_weight: bfloat16 [640, 1280], P('tm'), may hold values from -0.25 to 0.25
Outputs:
- block_out: bfloat16 [2, 48, 64, 1280], P('dp', 'tm')
- grad_tokens: bfloat16 [2, 48, 64, 1280], P('dp', 'tm')
- grad_output_weight: float32 [640, 1280], P('tm')
Inputs may be any that keep to these rules, and one draw needn't show every extreme that they name: visible[c, f, g] names which of the 3 cells of group g is visible in frame f.
All inputs are finite; a program needn't handle non-finite values.
Results may differ from a plain program's by a relative error of at most 0.012.
Values may be sent and summed in bfloat16 or wider, within the bound.
A program may use at most 64 MiB of HBM per device.

v0:
```python
import math

import jax
import jax.numpy as jnp
from jax import lax
from jax.experimental import pallas as pl
from jax.experimental.pallas import tpu as pltpu
from jax.sharding import PartitionSpec as P

HEADS = 8


NORM_EPS = 1e-06


def normalize(token_rows, norm_gain):
    values = token_rows.astype(jnp.float32)
    centered = values - jnp.mean(values, axis=-1, keepdims=True)
    inverse = lax.rsqrt(jnp.mean(centered * centered, axis=-1, keepdims=True) + NORM_EPS)
    scaled = centered * inverse
    return (scaled, inverse, (scaled * norm_gain).astype(jnp.bfloat16))


def project(token_rows, weight):
    lead_shape = token_rows.shape[:-1]
    flat_rows = token_rows.reshape(-1, token_rows.shape[-1])
    result = jnp.dot(flat_rows, weight, preferred_element_type=jnp.float32)
    return result.astype(jnp.bfloat16).reshape(lead_shape + (weight.shape[1],))


def split_heads(values):
    return values.reshape(values.shape[:-1] + (HEADS, values.shape[-1] // HEADS))


def attend(query_rows, key_rows, value_rows, same_cell):
    score_scale = 1.0 / math.sqrt(query_rows.shape[-1] // HEADS)
    query_heads = split_heads(query_rows)
    key_heads = split_heads(key_rows)
    value_heads = split_heads(value_rows)
    scores = (
        jnp.einsum("fghe,tghe->ghft", query_heads, key_heads, preferred_element_type=jnp.float32)
        * score_scale
    )
    scores = jnp.where(same_cell[:, None], scores, -jnp.inf)
    row_top = jnp.max(scores, axis=-1, keepdims=True)
    expons = jnp.exp(scores - row_top)
    soft_probs = expons / jnp.sum(expons, axis=-1, keepdims=True)
    probs_low = soft_probs.astype(jnp.bfloat16)
    mixed_rows = jnp.einsum(
        "ghft,tghe->fghe", probs_low, value_heads, preferred_element_type=jnp.float32
    )
    return (soft_probs, probs_low, mixed_rows.reshape(query_rows.shape).astype(jnp.bfloat16))


def attend_back(query_rows, key_rows, value_rows, soft_probs, probs_low, grad_mixed):
    score_scale = 1.0 / math.sqrt(query_rows.shape[-1] // HEADS)
    query_heads = split_heads(query_rows)
    key_heads = split_heads(key_rows)
    value_heads = split_heads(value_rows)
    grad_heads = split_heads(grad_mixed)
    grad_probs = jnp.einsum(
        "fghe,tghe->ghft", grad_heads, value_heads, preferred_element_type=jnp.float32
    )
    centre = jnp.sum(soft_probs * grad_probs, axis=-1, keepdims=True)
    grad_scores = (soft_probs * (grad_probs - centre) * score_scale).astype(jnp.bfloat16)
    grad_query = jnp.einsum(
        "ghft,tghe->fghe", grad_scores, key_heads, preferred_element_type=jnp.float32
    )
    grad_key = jnp.einsum(
        "ghft,fghe->tghe", grad_scores, query_heads, preferred_element_type=jnp.float32
    )
    grad_value = jnp.einsum(
        "ghft,fghe->tghe", probs_low, grad_heads, preferred_element_type=jnp.float32
    )
    full_shape = query_rows.shape
    return (
        grad_query.reshape(full_shape).astype(jnp.bfloat16),
        grad_key.reshape(full_shape).astype(jnp.bfloat16),
        grad_value.reshape(full_shape).astype(jnp.bfloat16),
    )


def back_project(grad_query, grad_key, grad_value, query_weight, key_weight, value_weight):
    lead_shape = grad_query.shape[:-1]
    width = grad_query.shape[-1]
    total = jnp.dot(
        grad_query.reshape(-1, width), query_weight.T, preferred_element_type=jnp.float32
    )
    total = total + jnp.dot(
        grad_key.reshape(-1, width), key_weight.T, preferred_element_type=jnp.float32
    )
    total = total + jnp.dot(
        grad_value.reshape(-1, width), value_weight.T, preferred_element_type=jnp.float32
    )
    return total.astype(jnp.bfloat16).reshape(lead_shape + (query_weight.shape[0],))


def on_device(
    frame_tokens,
    visible,
    grad_output,
    norm_gain,
    query_weight,
    key_weight,
    value_weight,
    output_weight,
):
    query_weight, key_weight, value_weight, output_weight = (
        lax.all_gather(query_weight, "tm", axis=0, tiled=True),
        lax.all_gather(key_weight, "tm", axis=0, tiled=True),
        lax.all_gather(value_weight, "tm", axis=0, tiled=True),
        lax.all_gather(output_weight, "tm", axis=0, tiled=True),
    )
    shards = lax.axis_size("tm")
    tokens = frame_tokens[0]
    frame_count, visible_count, width = tokens.shape
    att_width = output_weight.shape[0]
    groups = visible_count // shards
    scaled, inverse, normed = normalize(tokens, norm_gain)
    local_cells = lax.dynamic_slice_in_dim(visible[0], lax.axis_index("tm") * groups, groups, 1)
    cell_major = local_cells.T
    same_cell = cell_major[:, :, None] == cell_major[:, None, :]
    query_rows = project(normed, query_weight)
    key_rows = project(normed, key_weight)
    value_rows = project(normed, value_weight)
    query_rows, key_rows, value_rows = (
        lax.all_to_all(query_rows, "tm", split_axis=1, concat_axis=0, tiled=True),
        lax.all_to_all(key_rows, "tm", split_axis=1, concat_axis=0, tiled=True),
        lax.all_to_all(value_rows, "tm", split_axis=1, concat_axis=0, tiled=True),
    )
    soft_probs, probs_low, mixed_cells = attend(query_rows, key_rows, value_rows, same_cell)
    mixed_frames = lax.all_to_all(mixed_cells, "tm", split_axis=0, concat_axis=1, tiled=True)
    flat_mixed = mixed_frames.reshape(-1, att_width)
    flat_tokens = tokens.reshape(-1, width)
    update = jnp.dot(flat_mixed, output_weight, preferred_element_type=jnp.float32)
    block_rows = (
        (flat_tokens.astype(jnp.float32) + update).astype(jnp.bfloat16).reshape(tokens.shape)
    )
    flat_grad = grad_output[0].reshape(-1, width)
    grad_mixed = jnp.dot(flat_grad, output_weight.T, preferred_element_type=jnp.float32)
    grad_mixed = grad_mixed.astype(jnp.bfloat16).reshape(frame_count, visible_count, att_width)
    term_share = lax.psum_scatter(
        jnp.dot(flat_mixed.T, flat_grad, preferred_element_type=jnp.float32),
        "tm",
        scatter_dimension=0,
        tiled=True,
    )
    grad_weight = lax.psum(term_share.astype(jnp.bfloat16), "dp").astype(jnp.float32)
    grad_cells = lax.all_to_all(grad_mixed, "tm", split_axis=1, concat_axis=0, tiled=True)
    grad_query, grad_key, grad_value = attend_back(
        query_rows, key_rows, value_rows, soft_probs, probs_low, grad_cells
    )
    grad_query, grad_key, grad_value = (
        lax.all_to_all(grad_query, "tm", split_axis=0, concat_axis=1, tiled=True),
        lax.all_to_all(grad_key, "tm", split_axis=0, concat_axis=1, tiled=True),
        lax.all_to_all(grad_value, "tm", split_axis=0, concat_axis=1, tiled=True),
    )
    grad_normed = back_project(
        grad_query, grad_key, grad_value, query_weight, key_weight, value_weight
    )
    weighted = grad_normed.astype(jnp.float32) * norm_gain
    first_mean = jnp.mean(weighted, axis=-1, keepdims=True)
    second_mean = jnp.mean(weighted * scaled, axis=-1, keepdims=True)
    grad_rows = inverse * (weighted - first_mean - scaled * second_mean) + grad_output[0].astype(
        jnp.float32
    )
    return (block_rows[None], grad_rows.astype(jnp.bfloat16)[None], grad_weight)


SHARDS = 16
ROWS = 16


def nt_dot(left, right):
    return lax.dot_general(left, right, (((1,), (1,)), ((), ())), preferred_element_type=jnp.float32)


def tn_dot(left, right):
    return lax.dot_general(left, right, (((0,), (0,)), ((), ())), preferred_element_type=jnp.float32)


def nn_dot(left, right):
    return jnp.dot(left, right, preferred_element_type=jnp.float32)


def head_window(head, head_dim):
    low = head * head_dim
    start = low // 128 * 128
    stop = -(-(low + head_dim) // 128) * 128
    lane = lax.broadcasted_iota(jnp.int32, (1, stop - start), 1) + start
    inside = jnp.where((lane >= low) & (lane < low + head_dim), 1.0, 0.0)
    return (slice(start, stop), inside.astype(jnp.bfloat16))


def block_maps(cells, frames, frame_map, cell_map):
    groups = cells // SHARDS
    taken = frames * groups
    place = lax.broadcasted_iota(jnp.int32, (SHARDS * ROWS, 1), 0)
    source = lax.broadcasted_iota(jnp.int32, (1, frames * cells), 1)
    owner, inner = lax.div(place, ROWS), lax.rem(place, ROWS)
    frame, group = lax.div(inner, groups), lax.rem(inner, groups)
    main = inner < taken

    def hits(wanted, valid):
        return jnp.where(jnp.where(valid, wanted, -1) == source, 1.0, 0.0).astype(jnp.bfloat16)

    frame_map[0] = hits(frame * cells + owner * groups + group, main)
    cell_map[0] = hits(owner * taken + inner, main)
    for f in range(frames):
        spare = jnp.logical_not(main)
        frame_map[1 + f] = hits(f * cells + owner * groups + inner - taken, spare)
        cell_map[1 + f] = hits(owner * taken + f * groups + inner - taken, spare)


def fused_kernel(
    tok, gout, gain, code_row, wq, wk, wv, wo,
    block_o, gtok_o, dw_o,
    wall, frame_map, cell_map, norm_s, norm_r, q_s, k_s, v_s, gm_s, probs_s,
    acc_a, acc_b, acc_c, gm_out, gm_in, mix_s, mix_r, gn_s, gn_r,
    dwp, dw_in, dwa_s, dwa_r, dwb_s, dwb_r, dwf,
    w_send, w_recv, sib_send, sib_recv, gm_send, gm_recv, no_send, no_recv,
    mi_send, mi_recv, gn_send, gn_recv, da_send, da_recv, db_send, db_recv, pair_send, pair_recv,
):
    t = lax.axis_index("tm")
    c = lax.axis_index("dp")
    x = lax.rem(t, 2)
    y = lax.rem(lax.div(t, 2), 2)
    z = lax.div(t, 4)
    plane = lax.rem(t, 4)
    xn = t + 1 - 2 * x
    yn = t + 2 - 4 * y
    att = q_s.shape[1]
    frames, cells, width = tok.shape
    count = frames * cells
    depth = wq.shape[0]
    share = wo.shape[0]
    rows = SHARDS * ROWS
    head_dim = att // HEADS
    scale = 1.0 / math.sqrt(head_dim)
    low, high = jnp.bfloat16, jnp.float32

    def to_tm(src, dst, send, recv, peer):
        return pltpu.make_async_remote_copy(
            src_ref=src, dst_ref=dst, send_sem=send, recv_sem=recv,
            device_id={"tm": peer}, device_id_type=pl.DeviceIdType.MESH,
        )

    def to_pair(src, dst, send, recv):
        return pltpu.make_async_remote_copy(
            src_ref=src, dst_ref=dst, send_sem=send, recv_sem=recv,
            device_id={"dp": 1 - c}, device_id_type=pl.DeviceIdType.MESH,
        )

    barrier = pltpu.get_barrier_semaphore()

    @pl.loop(1, SHARDS)
    def _(d):
        pl.semaphore_signal(
            barrier, inc=1, device_id={"tm": lax.rem(t + d, SHARDS)},
            device_id_type=pl.DeviceIdType.MESH,
        )

    pl.semaphore_signal(
        barrier, inc=1, device_id={"dp": 1 - c}, device_id_type=pl.DeviceIdType.MESH
    )
    wall[0, t] = wq[...]
    wall[1, t] = wk[...]
    wall[2, t] = wv[...]
    output_rows = wo[...].astype(high)
    wall[3, t] = jnp.concatenate([output_rows[:, :att], output_rows[:, att:]], axis=0).astype(low)
    pl.semaphore_wait(barrier, SHARDS)

    def item(h, s):
        return wall.at[3 * c if h == 0 else 1 + c, s]

    def pass_item(h, s, peer, kind):
        slot = (h * 5 + kind) * 4 + lax.div(s, 4)
        return to_tm(item(h, s), item(h, s), w_send.at[slot], w_recv.at[h * SHARDS + s], peer)

    def wait_item(h, s):
        pass_item(h, s, xn, 0).wait_recv()

    def pair_item(h, s):
        slot = h * SHARDS + s
        return to_pair(item(h, s), item(h, s), sib_send.at[slot], sib_recv.at[slot])

    def go_up(h, s):
        @pl.when(z < 3)
        def _():
            pass_item(h, s, t + 4, 0).start()

    def go_down(h, s):
        @pl.when(z > 0)
        def _():
            pass_item(h, s, t - 4, 1).start()

    def go_across(h, s):
        pass_item(h, s, xn, 2).start()
        pass_item(h, s, yn, 3).start()

    def at_levels(k, action):
        if k == 0:
            action(t, None)
        else:
            @pl.when(z >= k)
            def _():
                action(t - 4 * k, go_up)

            @pl.when(z + k <= 3)
            def _():
                action(t + 4 * k, go_down)

    def from_column(h, k):
        def action(s, onward):
            wait_item(h, s)
            onward(h, s)
            go_across(h, s)

        at_levels(k, action)

    def from_plane(h, k):
        def action(s, _):
            level = s - plane
            from_x = level + lax.rem(xn, 4)
            from_y = level + lax.rem(yn, 4)
            wait_item(h, from_x)

            @pl.when(c == 0)
            def _():
                pass_item(h, from_x, yn, 4).start()

            wait_item(h, from_y)

            @pl.when(c == 1)
            def _():
                pass_item(h, from_y, xn, 4).start()


        at_levels(k, action)

    def pair_level(h, level):
        return to_pair(
            level_items(c, h, level), level_items(c, h, level),
            sib_send.at[h * SHARDS + level], sib_recv.at[h * SHARDS + level],
        )

    def level_items(core, h, level):
        return wall.at[3 * core if h == 0 else 1 + core, pl.ds(level, 4)]

    def from_across(h, k):
        def action(s, _):
            level = s - plane
            wait_item(h, level + 3 - plane)
            if k == 0:
                for d in range(1, 4):
                    pair_item(h, level + lax.rem(plane + d, 4)).start()
            else:
                pair_level(h, level).start()

        at_levels(k, action)

    def send_own(h):
        go_up(h, t)
        go_down(h, t)
        go_across(h, t)

    def wait_pair(h):
        def action(s, _):
            level = s - plane
            if s is t:
                for d in range(1, 4):
                    mate = level + lax.rem(plane + d, 4)
                    slot = h * SHARDS + mate
                    landed = wall.at[3 * (1 - c) if h == 0 else 2 - c, mate]
                    to_pair(landed, landed, sib_send.at[slot], sib_recv.at[slot]).wait_recv()
            else:
                slot = h * SHARDS + level
                landed = level_items(1 - c, h, level)
                to_pair(landed, landed, sib_send.at[slot], sib_recv.at[slot]).wait_recv()

        for k in range(4):
            at_levels(k, action)

    send_own(0)

    def send_peers(src, dst, send, recv):
        @pl.loop(1, SHARDS)
        def _(d):
            peer = lax.rem(t + d, SHARDS)
            to_tm(src.at[peer], dst.at[t], send.at[0], recv.at[0], peer).start()

        dst[t] = src[t]

    def wait_peers(src, dst, send, recv, sends):
        others = pl.ds(0, SHARDS - 1)
        copies = to_tm(src.at[others], dst.at[others], send.at[0], recv.at[0], xn)
        if sends:
            copies.wait_send()
        else:
            copies.wait_recv()

    block_maps(cells, frames, frame_map, cell_map)

    def pack(row_map, values, out):
        columns = values.shape[1]
        tail = columns // 5
        packed = nn_dot(row_map[0], values[:, : columns - tail])
        spare = [nn_dot(row_map[1 + f], values[:, columns - tail :]) for f in range(frames)]
        spare.append(jnp.zeros((rows, columns - tail - frames * tail), high))
        packed = packed + jnp.concatenate(spare, axis=1)
        out[...] = packed.astype(low).reshape(out.shape)

    def unpack(row_map, packed):
        columns = packed.shape[2] * 5 // 4
        tail = columns // 5
        values = packed[...].reshape(rows, columns - tail)
        main = tn_dot(row_map[0], values)
        last = sum(tn_dot(row_map[1 + f], values[:, f * tail : (f + 1) * tail]) for f in range(frames))
        return jnp.concatenate([main, last], axis=1)

    def norm_rows():
        values = tok[...].reshape(count, width).astype(high)
        centered = values - jnp.mean(values, axis=-1, keepdims=True)
        inverse = lax.rsqrt(jnp.mean(centered * centered, axis=-1, keepdims=True) + NORM_EPS)
        return (centered * inverse, inverse)

    gains = gain[...].reshape(1, width)
    pack(frame_map, (norm_rows()[0] * gains).astype(low), norm_s)
    send_peers(norm_s, norm_r, no_send, no_recv)

    from_column(0, 1)
    send_own(1)
    from_plane(0, 0)
    from_column(0, 2)
    from_column(1, 1)
    from_plane(0, 1)
    from_plane(1, 0)
    from_across(0, 0)
    from_column(0, 3)
    from_column(1, 2)
    from_plane(0, 2)
    from_plane(1, 1)
    from_across(0, 1)
    from_across(1, 0)
    from_column(1, 3)
    from_plane(0, 3)
    from_plane(1, 2)
    from_across(0, 2)
    from_across(1, 1)
    from_plane(1, 3)
    from_across(0, 3)
    wait_pair(0)

    def full(j):
        return wall[j].reshape(SHARDS * depth, att)

    def output_half(j):
        blocks = wall[3].astype(high)[:, j * share : (j + 1) * share]
        return blocks.reshape(SHARDS * share, att).astype(low)

    grads = gout[...].reshape(count, width)
    grad_mixed = nt_dot(grads[:, :att], output_half(0)) + nt_dot(grads[:, att:], output_half(1))
    pack(frame_map, grad_mixed.astype(low), gm_out)
    send_peers(gm_out, gm_in, gm_send, gm_recv)

    from_across(1, 2)
    from_across(1, 3)
    wait_peers(norm_s, norm_r, no_send, no_recv, False)
    normed = unpack(cell_map, norm_r).astype(low)
    q_s[...] = nn_dot(normed, full(0)).astype(low)
    wait_pair(1)
    k_s[...] = nn_dot(normed, full(1)).astype(low)
    v_s[...] = nn_dot(normed, full(2)).astype(low)

    codes = jnp.broadcast_to(code_row[...].astype(high), (rows, rows))
    same = (codes == codes.T)[:count, :count]
    acc_a[...] = jnp.zeros_like(acc_a)
    for head in range(HEADS):
        window, inside = head_window(head, head_dim)
        scores = nt_dot(q_s[:, window] * inside, k_s[:, window]) * scale
        scores = jnp.where(same, scores, -jnp.inf)
        expons = jnp.exp(scores - jnp.max(scores, axis=-1, keepdims=True))
        probs = expons * (1.0 / jnp.sum(expons, axis=-1, keepdims=True))
        probs_s[head] = probs
        acc_a[:, window] += nn_dot(probs.astype(low), v_s[:, window] * inside)
    pack(cell_map, acc_a[...].astype(low), mix_s)
    send_peers(mix_s, mix_r, mi_send, mi_recv)

    wait_peers(gm_out, gm_in, gm_send, gm_recv, False)
    gm_s[...] = unpack(cell_map, gm_in).astype(low)

    acc_a[...] = jnp.zeros_like(acc_a)
    acc_b[...] = jnp.zeros_like(acc_b)
    acc_c[...] = jnp.zeros_like(acc_c)
    def back_head(head):
        window, inside = head_window(head, head_dim)
        grad_head = gm_s[:, window] * inside
        probs = probs_s[head]
        grad_probs = nt_dot(grad_head, v_s[:, window])
        centre = jnp.sum(probs * grad_probs, axis=-1, keepdims=True)
        grad_scores = (probs * (grad_probs - centre) * scale).astype(low)
        acc_a[:, window] += nn_dot(grad_scores, k_s[:, window] * inside)
        acc_b[:, window] += tn_dot(grad_scores, q_s[:, window] * inside)
        acc_c[:, window] += tn_dot(probs.astype(low), grad_head)

    for head in range(HEADS // 2):
        back_head(head)

    wait_peers(mix_s, mix_r, mi_send, mi_recv, False)
    mixed_frames = unpack(frame_map, mix_r).astype(low)
    for j in range(2):
        term = tn_dot(mixed_frames, grads[:, j * att : (j + 1) * att])
        term = term.reshape(4, 4, share, att).astype(low)
        for level in range(4):
            for place in range(4):
                dwp[j, place, level] = term[level, place]
    pair_term = to_pair(dwp.at[1 - c], dw_in, pair_send.at[0], pair_recv.at[0])
    pair_term.start()

    for head in range(HEADS // 2, HEADS):
        back_head(head)

    def mate_copy(d):
        mate = lax.rem(plane + d, 4)
        return to_tm(dwa_s.at[mate], dwa_r.at[plane], da_send.at[mate], da_recv.at[plane], z * 4 + mate)

    pair_term.wait_recv()

    @pl.loop(0, 4)
    def _(place):
        both = dwp[c, place].astype(high) + dw_in[place].astype(high)
        dwa_s[place] = both.astype(low)

    for d in range(1, 4):
        mate_copy(d).start()
    dwa_r[plane] = dwa_s[plane]

    grad_rows = [acc[...].astype(low) for acc in (acc_a, acc_b, acc_c)]
    for j in range(2):
        shards = slice(j * SHARDS // 2, (j + 1) * SHARDS // 2)
        total = sum(
            nt_dot(grad_rows[i], wall[i, shards].reshape(SHARDS // 2 * depth, att)) for i in range(3)
        )
        pack(cell_map, total.astype(low), gn_s.at[j])
        send_peers(gn_s.at[j], gn_r.at[j], gn_send.at[pl.ds(j, 1)], gn_recv.at[pl.ds(j, 1)])

    for j in range(2):
        columns = slice(j * att, (j + 1) * att)
        update = nn_dot(mixed_frames, output_half(j))
        rows_out = tok[:, :, columns].reshape(count, att).astype(high) + update
        block_o[:, :, columns] = rows_out.astype(low).reshape(frames, cells, att)
    scaled, inverse = norm_rows()

    def finish_items(h):
        pass_item(h, t, xn, 2).wait_send()
        pass_item(h, t, yn, 3).wait_send()
        for level in range(4):
            @pl.when((z < 3) & (level <= z))
            def _():
                pass_item(h, level * 4 + plane, xn, 0).wait_send()

            @pl.when((z > 0) & (level >= z))
            def _():
                pass_item(h, level * 4 + plane, xn, 1).wait_send()

            @pl.when(level != z)
            def _():
                pass_item(h, level * 4 + plane, xn, 2).wait_send()
                pass_item(h, level * 4 + plane, yn, 3).wait_send()
                pair_level(h, level * 4).wait_send()

            pass_item(h, level * 4 + plane, xn, 4).wait_send()
        for d in range(1, 4):
            pair_item(h, z * 4 + lax.rem(plane + d, 4)).wait_send()

    def level_copy(d):
        level = lax.rem(z + d, 4)
        return to_tm(dwb_s.at[level], dwb_r.at[z], db_send.at[level], db_recv.at[z], level * 4 + plane)

    for d in range(1, 4):
        mate = lax.rem(plane + d, 4)
        to_tm(dwa_s.at[mate], dwa_r.at[mate], da_send.at[mate], da_recv.at[mate], z * 4 + mate).wait_recv()
    dwb_s[...] = jnp.sum(dwa_r[...].astype(high), axis=0).astype(low)
    for d in range(1, 4):
        level_copy(d).start()
    dwb_r[z] = dwb_s[z]

    pair_term.wait_send()
    for h in range(2):
        finish_items(h)
    for d in range(1, 4):
        mate_copy(d).wait_send()
    wait_peers(gm_out, gm_in, gm_send, gm_recv, True)
    wait_peers(norm_s, norm_r, no_send, no_recv, True)
    wait_peers(mix_s, mix_r, mi_send, mi_recv, True)

    grad_parts = []
    for j in range(2):
        sems = (gn_send.at[pl.ds(j, 1)], gn_recv.at[pl.ds(j, 1)])
        wait_peers(gn_s.at[j], gn_r.at[j], *sems, False)
        grad_parts.append(unpack(frame_map, gn_r.at[j]))
    weighted = jnp.concatenate(grad_parts, axis=1) * gains
    first = jnp.mean(weighted, axis=-1, keepdims=True)
    second = jnp.mean(weighted * scaled, axis=-1, keepdims=True)
    result = inverse * (weighted - first - scaled * second)
    result = result + gout[...].reshape(count, width).astype(high)
    gtok_o[...] = result.astype(low).reshape(frames, cells, width)

    for d in range(1, 4):
        level = lax.rem(z + d, 4)
        to_tm(dwb_s.at[level], dwb_r.at[level], db_send.at[level], db_recv.at[level], level * 4 + plane).wait_recv()
    dwf[c] = jnp.sum(dwb_r[...].astype(high), axis=0)
    pair_sum = to_pair(dwf.at[c], dwf.at[c], pair_send.at[1], pair_recv.at[1])
    pair_sum.start()

    to_pair(dwf.at[1 - c], dwf.at[1 - c], pair_send.at[1], pair_recv.at[1]).wait_recv()
    dw_o[:, :att] = dwf[0]
    dw_o[:, att:] = dwf[1]

    pair_sum.wait_send()
    for d in range(1, 4):
        level_copy(d).wait_send()
    for j in range(2):
        sems = (gn_send.at[pl.ds(j, 1)], gn_recv.at[pl.ds(j, 1)])
        wait_peers(gn_s.at[j], gn_r.at[j], *sems, True)


def copy_kernel(*refs):
    for source, target in zip(refs[:3], refs[3:]):
        target[...] = source[...]


def on_chip_grid(
    frame_tokens,
    visible,
    grad_output,
    norm_gain,
    query_weight,
    key_weight,
    value_weight,
    output_weight,
):
    tokens = frame_tokens[0]
    frames, cells, width = tokens.shape
    groups = cells // SHARDS
    depth, att = query_weight.shape
    share = output_weight.shape[0]
    local = lax.dynamic_slice_in_dim(visible[0], lax.axis_index("tm") * groups, groups, 1)
    codes = local + 4 * jnp.arange(groups, dtype=jnp.int32)[None]
    rows, count = SHARDS * ROWS, frames * cells
    codes = jnp.pad(codes.reshape(1, count), ((0, 0), (0, rows - count)), constant_values=-1)
    low, high = jnp.bfloat16, jnp.float32
    vmem = pl.BlockSpec(memory_space=pltpu.VMEM)
    dma = pltpu.SemaphoreType.DMA
    wide = pltpu.VMEM((SHARDS, ROWS, width * 4 // 5), low)
    thin = pltpu.VMEM((SHARDS, ROWS, att * 4 // 5), low)
    two_thin = pltpu.VMEM((2, SHARDS, ROWS, att * 4 // 5), low)
    plain = pltpu.VMEM((count, att), low)
    total = pltpu.VMEM((count, att), high)
    quarter = pltpu.VMEM((4, 4, share, att), low)
    block_rows, grad_rows, grad_weight = pl.pallas_call(
        fused_kernel,
        out_shape=(
            jax.ShapeDtypeStruct(tokens.shape, low),
            jax.ShapeDtypeStruct(tokens.shape, low),
            jax.ShapeDtypeStruct((share, width), high),
        ),
        in_specs=[vmem] * 8,
        out_specs=(vmem,) * 3,
        scratch_shapes=[
            pltpu.VMEM((4, SHARDS, depth, att), low),
            pltpu.VMEM((1 + frames, rows, count), low),
            pltpu.VMEM((1 + frames, rows, count), low),
            wide, wide,
            plain, plain, plain, plain,
            pltpu.VMEM((HEADS, count, count), high),
            total, total, total,
            thin, thin, thin, thin, two_thin, two_thin,
            pltpu.VMEM((2, 4, 4, share, att), low),
            quarter, quarter, quarter,
            pltpu.VMEM((4, share, att), low),
            pltpu.VMEM((4, share, att), low),
            pltpu.VMEM((2, share, att), high),
            dma((40,)),
            *[dma((2 * SHARDS,))] * 3,
            *[dma((1,))] * 6,
            *[dma((2,))] * 2,
            *[dma((4,))] * 4,
            dma((2,)),
            dma((2,)),
        ],
        compiler_params=pltpu.CompilerParams(
            collective_id=0, has_side_effects=True, vmem_limit_bytes=40 * 1024 * 1024
        ),
        name="temporal_block",
    )(
        tokens,
        grad_output[0],
        norm_gain,
        codes,
        query_weight,
        key_weight,
        value_weight,
        output_weight,
    )
    results = (block_rows, grad_rows, grad_weight)
    block_rows, grad_rows, grad_weight = pl.pallas_call(
        copy_kernel,
        out_shape=tuple(jax.ShapeDtypeStruct(r.shape, r.dtype) for r in results),
        in_specs=[vmem] * 3,
        out_specs=(vmem,) * 3,
        name="copy_results",
    )(*results)
    return (block_rows[None], grad_rows[None], grad_weight)


def solution(mesh):
    chip_grid = mesh.shape["tm"] == SHARDS and mesh.shape["dp"] == 2
    return jax.shard_map(
        on_chip_grid if chip_grid else on_device,
        mesh=mesh,
        in_specs=(
            P("dp", "tm", None, None),
            P("dp", None, None),
            P("dp", "tm", None, None),
            P(),
            P("tm", None),
            P("tm", None),
            P("tm", None),
            P("tm", None),
        ),
        out_specs=(P("dp", "tm", None, None), P("dp", "tm", None, None), P("tm", None)),
        check_vma=False,
    )
```

profile of v0, /device:TPU:29, one launch (start us, length us, event | category | flops | bytes accessed | tf_op | source)
XLA Modules:
  0.0 92.4 jit_solution(17102316674544036547)
XLA Ops:
  0.6 0.0 copy-start
  0.6 0.0 copy-start.6
  0.7 0.1 add.24
  0.8 0.6 copy-done
  1.4 0.1 constant_dynamic-slice_fusion
  1.4 0.0 copy-start.10
  1.4 0.1 dynamic_slice.6
  1.6 0.0 copy-done.6
  1.6 0.6 copy-done.10
  2.2 0.0 copy-start.3
  2.2 1.0 %copy-done.3 = bf16[1,3,64,1280]{3,2,1,0:T(8,128)(2,1)S(1)} copy-done((bf16[1,3,64,1280]{3,2,1,0:T(8,128)(2,1)S(1)}, bf16[1,3,64,1280]{3,2,1,0:T(8,128)(2,1)}, u32[]{:S(2)}) %copy-start.3) | copy-done | bytes 491544
  3.2 0.0 copy-start.4
  3.2 1.0 %copy-done.4 = bf16[1,3,64,1280]{3,2,1,0:T(8,128)(2,1)S(1)} copy-done((bf16[1,3,64,1280]{3,2,1,0:T(8,128)(2,1)S(1)}, bf16[1,3,64,1280]{3,2,1,0:T(8,128)(2,1)}, u32[]{:S(2)}) %copy-start.4) | copy-done | bytes 491544
  4.2 0.0 copy-start.7
  4.2 0.9 copy-done.7
  5.1 0.0 copy-start.8
  5.1 0.9 copy-done.8
  6.0 0.0 copy-start.9
  6.0 0.9 copy-done.9
  6.9 81.0 %temporal_block.1 = (bf16[3,64,1280]{2,1,0:T(8,128)(2,1)S(1)}, bf16[3,64,1280]{2,1,0:T(8,128)(2,1)S(1)}, f32[40,1280]{1,0:T(8,128)S(1)}) custom-call(bf16[3,64,1280]{2,1,0:T(8,128)(2,1)S(1)} %bitcast.4, bf16[3,64,1280]{2,1,0:T(8,128)(2,1)S(1)} %bitcast.5, f32[1280]{0:T(1024)S(1)} %copy-done.10, s32[1,256]{1,0:T(1,128)S(1)} %pad.4.code_row, ...), custom_call_target="tpu_custom_call" | custom-call | tf_op jit(solution)/shard_map/temporal_block/pallas_call | solution.py:661
  87.9 0.0 copy-start.1
  87.9 0.8 copy-done.1
  88.7 0.0 copy-start.2
  88.7 0.8 copy-done.2
  89.4 0.0 copy-start.5
  89.5 0.7 copy-done.5
  90.1 2.3 %copy_results.1 = (bf16[3,64,1280]{2,1,0:T(8,128)(2,1)}, bf16[3,64,1280]{2,1,0:T(8,128)(2,1)}, f32[40,1280]{1,0:T(8,128)}) custom-call(bf16[3,64,1280]{2,1,0:T(8,128)(2,1)} %copy-done.1, bf16[3,64,1280]{2,1,0:T(8,128)(2,1)} %copy-done.2, f32[40,1280]{1,0:T(8,128)} %copy-done.5), custom_call_target="tpu_custom_call" | custom-call | tf_op jit(solution)/shard_map/copy_results/pallas_call | solution.py:707
  (4 shorter events, 0.0 us)
Async XLA Ops:
  0.6 0.7 copy-start
  0.6 0.9 %copy-start.6 = (bf16[80,640]{1,0:T(8,128)(2,1)S(1)}, bf16[80,640]{1,0:T(8,128)(2,1)}, u32[]{:S(2)}) copy-start(bf16[80,640]{1,0:T(8,128)(2,1)} %wq.1) | copy-start | bytes 307204
  1.4 0.7 copy-start.10
  2.2 1.0 %copy-start.3 = (bf16[1,3,64,1280]{3,2,1,0:T(8,128)(2,1)S(1)}, bf16[1,3,64,1280]{3,2,1,0:T(8,128)(2,1)}, u32[]{:S(2)}) copy-start(bf16[1,3,64,1280]{3,2,1,0:T(8,128)(2,1)} %param.8) | copy-start | bytes 1474564
  3.2 1.0 %copy-start.4 = (bf16[1,3,64,1280]{3,2,1,0:T(8,128)(2,1)S(1)}, bf16[1,3,64,1280]{3,2,1,0:T(8,128)(2,1)}, u32[]{:S(2)}) copy-start(bf16[1,3,64,1280]{3,2,1,0:T(8,128)(2,1)} %param.10) | copy-start | bytes 1474564
  4.2 0.9 copy-start.7
  5.1 0.9 copy-start.8
  6.0 0.9 copy-start.9
  87.9 0.8 copy-start.1
  88.7 0.8 copy-start.2
  89.4 0.7 copy-start.5
where the time goes:
time: 92.8 us; the launch traced here: 92.4 us
  Pallas kernels  83.2 us (90%)
  local copies, waits for them, and re-layouts  8.43 us (9%)
    pallas_call x1, Pallas kernels, on_chip_grid(): pl.pallas_call(fused_kernel, out_shape=(jax.ShapeDtypeStruct(tokens.shape...  81 us
    unnamed x22, local copies, waits for them, and re-layouts  8.14 us
    pallas_call x1, Pallas kernels, on_chip_grid(): pl.pallas_call(copy_kernel, out_shape=tuple((jax.ShapeDtypeStruct(r.shape...  2.26 us

commit v1 on v0

--- a/solution.py
+++ b/solution.py
@@ -213,13 +213,13 @@
 
 
 def fused_kernel(
-    tok, gout, gain, code_row, wq, wk, wv, wo,
-    block_o, gtok_o, dw_o,
-    wall, frame_map, cell_map, norm_s, norm_r, q_s, k_s, v_s, gm_s, probs_s,
+    tok_h, gout_h, gain, code_row, wq, wk, wv, wo_h,
+    block_h, gtok_h, dw_h,
+    tok, gout, wo, block_o, gtok_o, dw_o, wall, frame_map, cell_map, norm_s, norm_r, q_s, k_s, v_s, gm_s, probs_s,
     acc_a, acc_b, acc_c, gm_out, gm_in, mix_s, mix_r, gn_s, gn_r,
     dwp, dw_in, dwa_s, dwa_r, dwb_s, dwb_r, dwf,
     w_send, w_recv, sib_send, sib_recv, gm_send, gm_recv, no_send, no_recv,
-    mi_send, mi_recv, gn_send, gn_recv, da_send, da_recv, db_send, db_recv, pair_send, pair_recv,
+    mi_send, mi_recv, gn_send, gn_recv, da_send, da_recv, db_send, db_recv, pair_send, pair_recv, load_sem, store_sem,
 ):
     t = lax.axis_index("tm")
     c = lax.axis_index("dp")
@@ -251,6 +251,18 @@
             device_id={"dp": 1 - c}, device_id_type=pl.DeviceIdType.MESH,
         )
 
+    own = [wall.at[j, t] for j in range(3)]
+    sources = (wq, wk, wv, wo_h, tok_h, gout_h)
+    loads = [
+        pltpu.make_async_copy(source, target, load_sem.at[i])
+        for i, (source, target) in enumerate(zip(sources, (*own, wo, tok, gout)))
+    ]
+    for load in loads:
+        load.start()
+    stores = [
+        pltpu.make_async_copy(source, target, store_sem.at[i])
+        for i, (source, target) in enumerate(((block_o, block_h), (gtok_o, gtok_h), (dw_o, dw_h)))
+    ]
     barrier = pltpu.get_barrier_semaphore()
 
     @pl.loop(1, SHARDS)
@@ -263,9 +275,8 @@
     pl.semaphore_signal(
         barrier, inc=1, device_id={"dp": 1 - c}, device_id_type=pl.DeviceIdType.MESH
     )
-    wall[0, t] = wq[...]
-    wall[1, t] = wk[...]
-    wall[2, t] = wv[...]
+    for load in loads[:4]:
+        load.wait()
     output_rows = wo[...].astype(high)
     wall[3, t] = jnp.concatenate([output_rows[:, :att], output_rows[:, att:]], axis=0).astype(low)
     pl.semaphore_wait(barrier, SHARDS)
@@ -425,6 +436,7 @@
         return (centered * inverse, inverse)
 
     gains = gain[...].reshape(1, width)
+    loads[4].wait()
     pack(frame_map, (norm_rows()[0] * gains).astype(low), norm_s)
     send_peers(norm_s, norm_r, no_send, no_recv)
 
@@ -458,6 +470,7 @@
         blocks = wall[3].astype(high)[:, j * share : (j + 1) * share]
         return blocks.reshape(SHARDS * share, att).astype(low)
 
+    loads[5].wait()
     grads = gout[...].reshape(count, width)
     grad_mixed = nt_dot(grads[:, :att], output_half(0)) + nt_dot(grads[:, att:], output_half(1))
     pack(frame_map, grad_mixed.astype(low), gm_out)
@@ -549,6 +562,7 @@
         update = nn_dot(mixed_frames, output_half(j))
         rows_out = tok[:, :, columns].reshape(count, att).astype(high) + update
         block_o[:, :, columns] = rows_out.astype(low).reshape(frames, cells, att)
+    stores[0].start()
     scaled, inverse = norm_rows()
 
     def finish_items(h):
@@ -605,6 +619,7 @@
     result = inverse * (weighted - first - scaled * second)
     result = result + gout[...].reshape(count, width).astype(high)
     gtok_o[...] = result.astype(low).reshape(frames, cells, width)
+    stores[1].start()
 
     for d in range(1, 4):
         level = lax.rem(z + d, 4)
@@ -616,6 +631,7 @@
     to_pair(dwf.at[1 - c], dwf.at[1 - c], pair_send.at[1], pair_recv.at[1]).wait_recv()
     dw_o[:, :att] = dwf[0]
     dw_o[:, att:] = dwf[1]
+    stores[2].start()
 
     pair_sum.wait_send()
     for d in range(1, 4):
@@ -623,11 +639,8 @@
     for j in range(2):
         sems = (gn_send.at[pl.ds(j, 1)], gn_recv.at[pl.ds(j, 1)])
         wait_peers(gn_s.at[j], gn_r.at[j], *sems, True)
-
-
-def copy_kernel(*refs):
-    for source, target in zip(refs[:3], refs[3:]):
-        target[...] = source[...]
+    for store in stores:
+        store.wait()
 
 
 def on_chip_grid(
@@ -651,6 +664,8 @@
     codes = jnp.pad(codes.reshape(1, count), ((0, 0), (0, rows - count)), constant_values=-1)
     low, high = jnp.bfloat16, jnp.float32
     vmem = pl.BlockSpec(memory_space=pltpu.VMEM)
+    anywhere = pl.BlockSpec(memory_space=pl.ANY)
+    like_tokens = pltpu.VMEM(tokens.shape, low)
     dma = pltpu.SemaphoreType.DMA
     wide = pltpu.VMEM((SHARDS, ROWS, width * 4 // 5), low)
     thin = pltpu.VMEM((SHARDS, ROWS, att * 4 // 5), low)
@@ -665,9 +680,13 @@
             jax.ShapeDtypeStruct(tokens.shape, low),
             jax.ShapeDtypeStruct((share, width), high),
         ),
-        in_specs=[vmem] * 8,
-        out_specs=(vmem,) * 3,
+        in_specs=[anywhere, anywhere, vmem, vmem, anywhere, anywhere, anywhere, anywhere],
+        out_specs=(anywhere,) * 3,
         scratch_shapes=[
+            like_tokens, like_tokens,
+            pltpu.VMEM((share, width), low),
+            like_tokens, like_tokens,
+            pltpu.VMEM((share, width), high),
             pltpu.VMEM((4, SHARDS, depth, att), low),
             pltpu.VMEM((1 + frames, rows, count), low),
             pltpu.VMEM((1 + frames, rows, count), low),
@@ -688,9 +707,11 @@
             *[dma((4,))] * 4,
             dma((2,)),
             dma((2,)),
+            dma((6,)),
+            dma((3,)),
         ],
         compiler_params=pltpu.CompilerParams(
-            collective_id=0, has_side_effects=True, vmem_limit_bytes=40 * 1024 * 1024
+            collective_id=0, has_side_effects=True, vmem_limit_bytes=56 * 1024 * 1024
         ),
         name="temporal_block",
     )(
@@ -703,14 +724,6 @@
         value_weight,
         output_weight,
     )
-    results = (block_rows, grad_rows, grad_weight)
-    block_rows, grad_rows, grad_weight = pl.pallas_call(
-        copy_kernel,
-        out_shape=tuple(jax.ShapeDtypeStruct(r.shape, r.dtype) for r in results),
-        in_specs=[vmem] * 3,
-        out_specs=(vmem,) * 3,
-        name="copy_results",
-    )(*results)
     return (block_rows[None], grad_rows[None], grad_weight)
 
 

time: 92.8 us -> 88.5 us (0.954)
  local copies, waits for them, and re-layouts: 8.43 us -> 5.14 us
    unnamed x22 -> x9, local copies, waits for them, and re-layouts: 8.14 us -> 4.29 us
    pallas_call x1 -> x0, Pallas kernels: 2.26 us -> none  [on_chip_grid(): pl.pallas_call(copy_kernel, out_shape=tuple((jax.ShapeDtypeStruct(r.shape...]
    pallas_call x1, Pallas kernels: 81 us -> 82.4 us  [on_chip_grid(): pl.pallas_call(fused_kernel, out_shape=(jax.ShapeDtypeStruct(tokens.shape...]
where the time goes in v1:
time: 88.5 us; the launch traced here: 88.2 us
  Pallas kernels  82.4 us (93%)
  local copies, waits for them, and re-layouts  5.14 us (6%)
    pallas_call x1, Pallas kernels, on_chip_grid(): pl.pallas_call(fused_kernel, out_shape=(jax.ShapeDtypeStruct(tokens.shape...  82.4 us
    unnamed x9, local copies, waits for them, and re-layouts  4.29 us

profile of v1, /device:TPU:29, one launch (start us, length us, event | category | flops | bytes accessed | tf_op | source)
XLA Modules:
  0.0 88.2 jit_solution(7373862023964787024)
XLA Ops:
  0.6 0.0 copy-start
  0.7 0.1 add.24
  0.8 0.6 copy-done
  1.4 0.1 constant_dynamic-slice_fusion
  1.4 0.1 dynamic_slice.6
  1.6 0.6 pad.4.code_row
  2.1 82.4 %temporal_block.1 = (bf16[3,64,1280]{2,1,0:T(8,128)(2,1)}, bf16[3,64,1280]{2,1,0:T(8,128)(2,1)}, f32[40,1280]{1,0:T(8,128)}) custom-call(bf16[3,64,1280]{2,1,0:T(8,128)(2,1)} %bitcast.4, bf16[3,64,1280]{2,1,0:T(8,128)(2,1)} %bitcast.5, f32[1280]{0:T(1024)} %gain.1, s32[1,256]{1,0:T(1,128)} %pad.4.code_row, bf16[80,640]{1,0:T(8,128)(2,1)} %wq.1, ...), custom_call_target="tpu_custom_call" | custom-call | tf_op jit(solution)/shard_map/temporal_block/pallas_call | solution.py:676
  84.5 0.0 copy-start.1
  84.5 1.9 %copy.14 = bf16[1,3,64,1280]{3,2,1,0:T(8,128)(2,1)} copy(bf16[1,3,64,1280]{3,2,1,0:T(8,128)(2,1)} %bitcast.7) | data formatting | bytes 983040
  86.4 0.0 copy-done.1
  86.4 0.0 copy-start.2
  86.4 0.8 copy.15
  87.2 0.3 copy-done.2
  87.6 0.7 copy.16
  (3 shorter events, 0.0 us)
Async XLA Ops:
  0.6 0.7 copy-start
  84.5 1.9 %copy-start.1 = (bf16[3,64,1280]{2,1,0:T(8,128)(2,1)S(1)}, bf16[3,64,1280]{2,1,0:T(8,128)(2,1)}, u32[]{:S(2)}) copy-start(bf16[3,64,1280]{2,1,0:T(8,128)(2,1)} %get-tuple-element.7) | copy-start | bytes 1474564
  86.4 1.1 %copy-start.2 = (f32[40,1280]{1,0:T(8,128)S(1)}, f32[40,1280]{1,0:T(8,128)}, u32[]{:S(2)}) copy-start(f32[40,1280]{1,0:T(8,128)} %get-tuple-element.14) | copy-start | bytes 614404
